TPU v7x, 128 devices: a whole 4x4x4 slice. The times are simulated.
128 devices in a mesh: ctx: 16 (over z, x_hi, core), head: 8 (over y, x_lo).
Axes of the slice: x: 4 (x_hi: 2, x_lo: 2; x = x_hi * 2 + x_lo), y: 4, z: 4, core: 2. Of those that a mesh axis runs over, the one named last changes fastest.
Arguments:
- queries: bfloat16 [2048, 8192], P('ctx', 'head'), may hold values from -17.5 to 17.5
- incoming_keys: bfloat16 [2048, 1024], P('ctx', 'head'), may hold values from -7.5 to 7.5
- incoming_values: bfloat16 [2048, 1024], P('ctx', 'head'), may hold values from -6 to 6
- paged_key_cache: bfloat16 [256, 8, 128, 128], P('ctx', 'head'), may hold values from -7.5 to 7.5
- paged_value_cache: bfloat16 [256, 8, 128, 128], P('ctx', 'head'), may hold values from -6 to 6
- block_table: int32 [4, 64], replicated, may hold values from 0 to 255, as said below
- cache_len: int32 [4], replicated, may hold values from 2048 to 8192
- new_start: int32 [5], replicated, may hold values from 0 to 2048, as said below
- out_weight: bfloat16 [8192, 8192], P('head'), may hold values from -0.09375 to 0.09375
Outputs:
- mixed: bfloat16 [2048, 8192], P('ctx', 'head')
Inputs may be any that keep to these rules, and one draw needn't show every extreme that they name: `block_table`: each page slot appears exactly once; row r lists the page slots of request r's pages in order. Rises strictly from new_start[0] = 0 to new_start[4] = 2048.
All inputs are finite; a program needn't handle non-finite values.
Results may differ from a plain program's by a relative error of at most 0.0055.
Values may be sent and summed in bfloat16 or wider, within the bound.
No kernel may reach another device: no remote copies, remote signals or barrier semaphores. Data moves between devices by JAX's collectives and lax.ppermute only.
A program may use at most 128 MiB of HBM per device.

v0:
```python
import functools
import math

import jax
import jax.numpy as jnp
from jax import lax
from jax.experimental import pallas as pl
from jax.experimental.pallas import tpu as pltpu
from jax.sharding import PartitionSpec as P

F32 = jnp.float32
BF16 = jnp.bfloat16
I32 = jnp.int32

MASKED = -1e30
LOWEST = -1e20
LIST = 64
TASKS = 128
FIELDS = 8
FAR = 1 << 20
VMEM_BYTES = 14 * 1024 * 1024
LARGE_VMEM_BYTES = 30 * 1024 * 1024
SMALL_VMEM_BYTES = 8 * 1024 * 1024


def smem():
    return pl.BlockSpec(memory_space=pltpu.SMEM)


def vmem():
    return pl.BlockSpec(memory_space=pltpu.VMEM)


def anywhere():
    return pl.BlockSpec(memory_space=pl.ANY)


def hbm():
    return pl.BlockSpec(memory_space=pltpu.HBM)


def plan_kernel(requests, blocks, page_size, me_ref, table_ref, len_ref, start_ref, *refs):
    outs, list_ref, count_ref = refs[:4], refs[4], refs[5]
    me = me_ref[0]
    whole_page = page_size * 256

    for r in range(requests):
        length = len_ref[r]
        full = length // page_size
        near_base, far_base = r * LIST, (requests + r) * LIST

        def pages(i, counts, r=r, full=full, near_base=near_base, far_base=far_base):
            near, far = counts
            for u in range(4):
                j = 4 * i + u
                slot = table_ref[r, j]
                relative = (slot >> 4) ^ me
                is_far = relative >= 2
                list_ref[jnp.where(is_far, far, near)] = (
                    (relative & 1) * (blocks + 1) + (slot & 15) + whole_page
                )
                one = jnp.where((relative < 4) & (j < full), 1, 0)
                far_one = jnp.where(is_far, one, 0)
                near, far = near + one - far_one, far + far_one
            return near, far

        near, far = lax.fori_loop(
            0, (full + 3) // 4, pages, (jnp.int32(near_base), jnp.int32(far_base))
        )
        slot = table_ref[r, jnp.minimum(full, table_ref.shape[1] - 1)]
        relative = (slot >> 4) ^ me
        live = length - full * page_size
        is_far = relative >= 2
        list_ref[jnp.where(is_far, far, near)] = (
            (relative & 1) * (blocks + 1) + (slot & 15) + live * 256
        )
        one = jnp.where((relative < 4) & (live > 0), 1, 0)
        far_one = jnp.where(is_far, one, 0)
        count_ref[r] = near + one - far_one
        count_ref[requests + r] = far + far_one

    for out, phase, first_k, last_k in zip(outs, (0, 0, 1, 1), (0, 1, 0, 1), (1, 4, 1, 4)):

        def step(item, first, out=out, phase=phase, first_k=first_k):
            k, r = item // requests + first_k, item % requests
            number = ((me // 4 + 4 - k) % 4) * 4 + me % 4
            low = number * 128
            begin, end = start_ref[r], start_ref[r + 1]

            def add():
                which = phase * requests + r
                base = which * LIST
                total = count_ref[which]
                for side in range(2):
                    other = me ^ (2 * phase + side)
                    list_ref[total] = side * (blocks + 1) + blocks - (1 + other) * 256
                    meets = (other <= number) & (begin < other * 128 + 128) & (end > other * 128)
                    total = total + jnp.where(meets, 1, 0)
                list_ref[total] = 0
                pairs = (total - base + 1) // 2

                def task(i, _):
                    at = (first + i) * FIELDS
                    one, two = list_ref[base + 2 * i], list_ref[base + 2 * i + 1]
                    out[at] = k - first_k
                    out[at + 1] = one
                    out[at + 2] = two
                    out[at + 3] = jnp.where((one >> 8 == page_size) & (two >> 8 == page_size), 0, 1)
                    out[at + 4] = low
                    out[at + 5] = r
                    return 0

                lax.fori_loop(0, pairs, task, 0)
                return first + pairs

            return lax.cond((begin < low + 128) & (end > low), add, lambda: first)

        last = lax.fori_loop(0, (last_k - first_k) * requests, step, jnp.int32(0))
        out[TASKS * FIELDS] = last
        for extra in range(2):
            for field in range(FIELDS):
                out[(last + extra) * FIELDS + field] = 1 if field == 3 else 0


def make_plan(me, block_table, cache_len, new_start, blocks, page_size):
    requests = block_table.shape[0]
    return pl.pallas_call(
        functools.partial(plan_kernel, requests, blocks, page_size),
        out_shape=[pltpu.SMEM((TASKS * FIELDS + 128,), I32)] * 4,
        in_specs=[smem()] * 4,
        out_specs=[smem()] * 4,
        scratch_shapes=[
            pltpu.SMEM((2 * requests * LIST,), I32),
            pltpu.SMEM((2 * requests,), I32),
        ],
        cost_estimate=pl.CostEstimate(flops=1_000_000_000, bytes_accessed=100_000, transcendentals=0),
        name="plan",
    )(me, block_table, cache_len, new_start)


def run_tasks(plan_ref, start_ref, qt_ref, keys_ref, values_ref, scores_ref, acc_ref, high_ref, sum_ref, scale, width, ready):
    columns = qt_ref.shape[2]
    starts = list(range(0, columns, width))

    def place_of(entry):
        return entry & 255

    def score(task, place):
        at = task * FIELDS
        k = plan_ref[at]
        key_block = jnp.concatenate(
            [keys_ref[place_of(plan_ref[at + 1])], keys_ref[place_of(plan_ref[at + 2])]], axis=0
        )
        for c in starts:
            scores_ref[place, :, c : c + width] = jnp.dot(
                key_block, qt_ref[k, :, c : c + width], preferred_element_type=F32
            )

    def absorb(task, place, masked):
        at = task * FIELDS
        k, one, two = plan_ref[at], plan_ref[at + 1], plan_ref[at + 2]
        value_block = jnp.concatenate([values_ref[place_of(one)].T, values_ref[place_of(two)].T], axis=1)
        value_block = jnp.concatenate([value_block, jnp.ones((16, 256), BF16)], axis=0)
        low, r = plan_ref[at + 4], plan_ref[at + 5]
        begin, end = start_ref[r], start_ref[r + 1]
        token = low + lax.broadcasted_iota(I32, (1, width), 1) % 128
        inside = (token >= begin) & (token < end)
        if masked:
            row = lax.broadcasted_iota(I32, (128, 1), 0)
            rows = []
            for entry in (one, two):
                code = entry >> 8
                key = row - (code + 1) * 128
                rows.append(
                    jnp.where(
                        code >= 0,
                        jnp.where(row < code, -1, FAR),
                        jnp.where((key >= begin) & (key < end), key, FAR),
                    )
                )
            key_token = jnp.concatenate(rows, axis=0)
        for c in starts:
            cols = slice(c, c + width)
            scores = scores_ref[place, :, cols]
            if masked:
                scores = jnp.where(key_token <= token, scores, MASKED)
            before = high_ref[k, :, cols]
            high = jnp.where(inside, jnp.maximum(before, jnp.max(scores, axis=0, keepdims=True)), before)
            weights = jnp.exp2(scores * scale - jnp.where(inside, high * scale, -MASKED))
            shrink = jnp.exp2((before - high) * scale)
            part = jnp.dot(value_block, weights.astype(BF16), preferred_element_type=F32)
            high_ref[k, :, cols] = high
            sum_ref[k, :, cols] = sum_ref[k, :, cols] * shrink + part[128:129]
            acc_ref[k, :, cols] = acc_ref[k, :, cols] * shrink + part[:128]

    def step(task, place):
        masked = plan_ref[task * FIELDS + 3]

        @pl.when(masked == 0)
        def _():
            score(task + 1, 1 - place)
            absorb(task, place, False)

        @pl.when(masked != 0)
        def _():
            score(task + 1, 1 - place)
            absorb(task, place, True)

    def two(i, _):
        step(2 * i, 0)
        step(2 * i + 1, 1)
        return 0

    score(0, 0)
    ready()
    lax.fori_loop(0, (plan_ref[TASKS * FIELDS] + 1) // 2, two, 0)


def clear(acc_ref, high_ref, sum_ref):
    acc_ref[...] = jnp.zeros(acc_ref.shape, F32)
    high_ref[...] = jnp.full(high_ref.shape, LOWEST, F32)
    sum_ref[...] = jnp.zeros(sum_ref.shape, F32)


def bring(targets_ref, source_ref, outs, sems, wide):
    pieces = 2
    step = source_ref.shape[0] // pieces
    copies = []
    for n, out in enumerate(outs):
        at = pl.multiple_of(targets_ref[n] * wide, wide)
        for p in range(pieces):
            rows = pl.ds(p * step, step)
            copies.append(
                pltpu.make_async_copy(
                    source_ref.at[rows, pl.ds(at, wide)], out.at[rows], sems.at[n * pieces + p]
                )
            )
            copies[-1].start()
    return copies


def attend_kernel(form, *refs):
    refs = list(refs)

    def take(n):
        taken = refs[:n]
        del refs[:n]
        return taken

    count, blocks, scale = form["count"], form["blocks"], form["scale"]
    first, last, wide, weights = form["first"], form["last"], form["wide"], form["weights"]
    plan_ref, start_ref = take(2)
    sets = take(form["sets"])
    if first:
        query_refs = take(count)
    else:
        qt_in, *state_in = take(4)
    if weights:
        targets_ref, weight_ref = take(2)
    if last:
        message_refs = take(count)
    else:
        qt_out, *state_out = take(4)
    block_refs = take(weights)
    qt_ref, keys_ref, values_ref, scores_ref = take(4)
    state = take(3)
    if first:
        q_ref = take(1)[0]
    else:
        earlier = take(3)
    key_sems, query_sems, state_sems, weight_sems = take(4)
    acc_ref, high_ref, sum_ref = state
    columns = qt_ref.shape[2]
    heads = columns // 128

    queries = []
    if first:
        for k, ref in enumerate(query_refs):
            queries.append(pltpu.make_async_copy(ref, q_ref.at[k], query_sems.at[k]))
    else:
        queries.append(pltpu.make_async_copy(qt_in, qt_ref, query_sems.at[0]))
    key_copies, value_copies, state_copies = [], [], []
    for n, ref in enumerate(sets):
        to = pl.ds(n * blocks, blocks)
        key_copies.append(
            pltpu.make_async_copy(ref.at[pl.ds(0, blocks)], keys_ref.at[to], key_sems.at[2 * n])
        )
        value_copies.append(
            pltpu.make_async_copy(ref.at[pl.ds(blocks, blocks)], values_ref.at[to], key_sems.at[2 * n + 1])
        )
    if not first:
        for n, (source, target) in enumerate(zip(state_in, earlier)):
            state_copies.append(pltpu.make_async_copy(source, target, state_sems.at[n]))
    for copy in queries + key_copies + value_copies + state_copies:
        copy.start()
    brought = bring(targets_ref, weight_ref, block_refs, weight_sems, wide) if weights else []
    clear(acc_ref, high_ref, sum_ref)
    for k, copy in enumerate(queries):
        copy.wait()
        if first:
            for c in range(0, columns, 128):
                qt_ref[k, :, c : c + 128] = q_ref[k, :, c : c + 128].T
    outgoing = []
    if not last:
        outgoing.append(pltpu.make_async_copy(qt_ref, qt_out, query_sems.at[count]))
        outgoing[0].start()
    for copy in key_copies:
        copy.wait()

    def ready():
        for copy in value_copies:
            copy.wait()

    run_tasks(
        plan_ref, start_ref, qt_ref, keys_ref, values_ref, scores_ref, acc_ref, high_ref, sum_ref, scale, 256, ready
    )

    for copy in state_copies:
        copy.wait()
    if not last:
        for n, (source, target) in enumerate(zip(state, state_out)):
            outgoing.append(pltpu.make_async_copy(source, target, state_sems.at[n]))
            outgoing[-1].start()
        for copy in outgoing:
            copy.wait()
        return

    for k in range(count):
        if first:
            high = high_ref[k]
            total = sum_ref[k]
        else:
            acc_a, high_a, sum_a = earlier
            high = jnp.maximum(high_ref[k], high_a[k])
            shrink_a = jnp.exp2((high_a[k] - high) * scale)
            shrink = jnp.exp2((high_ref[k] - high) * scale)
            total = sum_a[k] * shrink_a + sum_ref[k] * shrink
        some = total > 0.0
        safe = jnp.where(some, total, 1.0)
        inverse = jnp.where(some, 1.0 / safe, 0.0)
        level = jnp.where(some, high * scale + jnp.log2(safe), MASKED)
        if not first:
            factor_a, factor = shrink_a * inverse, shrink * inverse
        levels = []
        for h in range(heads):
            cols = slice(h * 128, (h + 1) * 128)
            if first:
                value = acc_ref[k, :, cols] * inverse[:, cols]
            else:
                value = acc_a[k, :, cols] * factor_a[:, cols] + acc_ref[k, :, cols] * factor[:, cols]
            message_refs[k][cols, :] = value.astype(BF16)
            levels.append(level[:, cols])
        level = jnp.concatenate(levels, axis=0)
        one = level.astype(BF16)
        rest = level - one.astype(F32)
        two = rest.astype(BF16)
        three = (rest - two.astype(F32)).astype(BF16)
        tail = jnp.concatenate(
            [one.astype(F32), two.astype(F32), three.astype(F32), jnp.zeros_like(level)], axis=0
        )
        message_refs[k][heads * 128 :, :] = tail.astype(BF16)
    for copy in brought:
        copy.wait()


def attend(plan, new_start, sets, scale, queries=None, state=None, last=False, targets=None, weight=None, wide=0, name="attend"):
    first = state is None
    if first:
        count, columns = len(queries), queries[0].shape[1]
    else:
        count, _, columns = state[0].shape
    blocks = sets[0].shape[0] // 2
    weights = 0 if targets is None else targets.shape[0]
    state_shapes = [(count, 128, columns), (count, 1, columns), (count, 1, columns)]
    rows = columns + 4 * (columns // 128)
    form = dict(
        count=count, blocks=blocks, scale=scale, sets=len(sets), first=first, last=last, wide=wide, weights=weights
    )
    in_specs = [smem()] * 2 + [anywhere()] * len(sets)
    inputs = [plan, new_start, *sets]
    if first:
        in_specs += [anywhere()] * count
        inputs += queries
    else:
        in_specs += [hbm()] * 4
        inputs += [pltpu.with_memory_space_constraint(x, pltpu.HBM) for x in state]
    if weights:
        in_specs += [smem(), anywhere()]
        inputs += [targets, weight]
    if last:
        out_shape = [jax.ShapeDtypeStruct((rows, 128), BF16)] * count
        out_specs = [vmem()] * count
    else:
        out_shape = [pltpu.HBM((count, 128, columns), BF16)]
        out_shape += [pltpu.HBM(s, F32) for s in state_shapes]
        out_specs = [hbm()] * 4
    out_shape += [jax.ShapeDtypeStruct((weight.shape[0], wide), weight.dtype) for _ in range(weights)]
    out_specs += [vmem()] * weights
    states = [pltpu.VMEM(s, F32) for s in state_shapes]
    scratch = [
        pltpu.VMEM((count, 128, columns), BF16),
        pltpu.VMEM((len(sets) * blocks, 128, 128), BF16),
        pltpu.VMEM((len(sets) * blocks, 128, 128), BF16),
        pltpu.VMEM((2, 256, columns), F32),
    ]
    scratch += states + ([pltpu.VMEM((count, 128, columns), BF16)] if first else states)
    scratch += [
        pltpu.SemaphoreType.DMA((2 * len(sets),)),
        pltpu.SemaphoreType.DMA((count + 1,)),
        pltpu.SemaphoreType.DMA((3,)),
        pltpu.SemaphoreType.DMA((2 * max(weights, 1),)),
    ]
    return pl.pallas_call(
        functools.partial(attend_kernel, form),
        out_shape=out_shape,
        in_specs=in_specs,
        out_specs=out_specs,
        scratch_shapes=scratch,
        compiler_params=pltpu.CompilerParams(
            vmem_limit_bytes=LARGE_VMEM_BYTES if weights else VMEM_BYTES
        ),
        cost_estimate=pl.CostEstimate(
            flops=2_000_000_000, bytes_accessed=100_000, transcendentals=0
        ),
        name=name,
    )(*inputs)


def merged(messages, heads, out_ref):
    tails = [m[heads * 128 :, :].astype(F32) for m in messages]
    levels = [t[:heads] + t[heads : 2 * heads] + t[2 * heads : 3 * heads] for t in tails]
    top = functools.reduce(jnp.maximum, levels)
    weights = [jnp.exp2(level - top) for level in levels]
    total = functools.reduce(jnp.add, weights)
    weights = [w / total for w in weights]
    for h in range(heads):
        rows = slice(h * 128, (h + 1) * 128)
        value = sum(m[rows, :].astype(F32) * w[h : h + 1, :] for m, w in zip(messages, weights))
        out_ref[:, rows] = value.T.astype(BF16)


def merge_kernel(heads, *refs):
    merged(refs[:4], heads, refs[4])


def merge(messages, heads):
    return pl.pallas_call(
        functools.partial(merge_kernel, heads),
        out_shape=jax.ShapeDtypeStruct((128, heads * 128), BF16),
        in_specs=[vmem()] * 4,
        out_specs=vmem(),
        compiler_params=pltpu.CompilerParams(vmem_limit_bytes=SMALL_VMEM_BYTES),
        cost_estimate=pl.CostEstimate(flops=2_000_000, bytes_accessed=1_300_000, transcendentals=4096),
        name="merge",
    )(*messages)


def project_kernel(x_ref, w_ref, out_ref):
    out_ref[...] = jnp.dot(x_ref[...], w_ref[...], preferred_element_type=F32).astype(out_ref.dtype)


def project(attended, weight, dtype):
    rows, depth = attended.shape
    wide = weight.shape[1]
    return pl.pallas_call(
        project_kernel,
        out_shape=jax.ShapeDtypeStruct((rows, wide), dtype),
        in_specs=[vmem()] * 2,
        out_specs=vmem(),
        compiler_params=pltpu.CompilerParams(vmem_limit_bytes=SMALL_VMEM_BYTES),
        cost_estimate=pl.CostEstimate(
            flops=2 * rows * depth * wide, bytes_accessed=2 * depth * wide, transcendentals=0
        ),
        name="project",
    )(attended, weight)


def swap(value, axis, mask):
    return lax.ppermute(value, axis, [(i, i ^ mask) for i in range(lax.axis_size(axis))])


def forward(value, axis, by):
    count = lax.axis_size(axis)
    return lax.ppermute(value, axis, [(i, (i + by) % count) for i in range(count)])


def on_device(
    queries,
    incoming_keys,
    incoming_values,
    paged_key_cache,
    paged_value_cache,
    block_table,
    cache_len,
    new_start,
    out_weight,
):
    position = lax.axis_index("ctx")
    column = lax.axis_index("head")
    head_count = lax.axis_size("head")
    blocks = paged_key_cache.shape[0]
    page_size, head_width = paged_key_cache.shape[2:]
    scale = math.log2(math.e) / math.sqrt(head_width)
    wide = out_weight.shape[1] // head_count
    masks = (1, 6, 2, 7, 3, 4, 5)
    me = position.astype(I32).reshape(1)

    def as_blocks(value):
        return value.reshape(-1, page_size, head_width)

    own = jnp.concatenate(
        [as_blocks(v) for v in (paged_key_cache, incoming_keys, paged_value_cache, incoming_values)], axis=0
    )
    far = swap(own, "ctx", 2)
    near = swap(own, "ctx", 1)
    others = [forward(queries, "ctx", 4 * k) for k in range(1, 4)]
    near_own, near_others, far_own, far_others = make_plan(
        me, block_table, cache_len, new_start, blocks, page_size
    )
    state = attend(near_own, new_start, [own, near], scale, queries=[queries], name="attend_near_own")
    near_others, state = lax.optimization_barrier((near_others, state))
    others_state = attend(near_others, new_start, [own, near], scale, queries=others, name="attend_near")
    far, others_state = lax.optimization_barrier((far, others_state))
    far_near = swap(far, "ctx", 1)
    messages = attend(
        far_others, new_start, [far, far_near], scale, state=others_state, last=True, name="attend_far"
    )
    out_weight, far_own, *messages = lax.optimization_barrier([out_weight, far_own, *messages])
    message, *weights = attend(
        far_own, new_start, [far, far_near], scale, state=state, last=True,
        targets=column ^ jnp.array(masks + (0,), I32), weight=out_weight, wide=wide, name="attend_far_own",
    )
    received = [message] + [forward(m, "ctx", -4 * k) for k, m in zip((2, 1, 3), [messages[1], messages[0], messages[2]])]

    attended = merge(received, queries.shape[1] // head_width)
    shares = {}
    for mask, weight, after in zip(masks, weights, (None,) * 5 + masks[:2]):
        given = attended
        if after:
            given, shares[after] = lax.optimization_barrier((attended, shares[after]))
        shares[mask] = swap(project(given, weight, BF16), "head", mask)
    total = project(attended, weights[-1], F32)
    for mask in masks[:5]:
        total = total + shares[mask].astype(F32)
    total = lax.optimization_barrier(total)
    for mask in masks[5:]:
        total = total + shares[mask].astype(F32)
    return total.astype(BF16)


def solution(mesh):
    return jax.shard_map(
        on_device,
        mesh=mesh,
        in_specs=(
            P("ctx", "head"),
            P("ctx", "head"),
            P("ctx", "head"),
            P("ctx", "head", None, None),
            P("ctx", "head", None, None),
            P(),
            P(),
            P(),
            P("head", None),
        ),
        out_specs=P("ctx", "head"),
        check_vma=False,
    )
```

profile of v0, /device:TPU:6, one launch (start us, length us, event | category | flops | bytes accessed | tf_op | source)
XLA Modules:
  0.0 95.7 jit_solution(17344519523636047392)
XLA Ops:
  0.0 1.4 %pad_maximum_fusion.refs_2_ = bf16[34,128,128]{2,1,0:T(8,128)(2,1)S(1)} fusion(bf16[1,128,128]{2,1,0:T(8,128)(2,1)} %bitcast.7, bf16[16,128,128]{2,1,0:T(8,128)(2,1)} %bitcast.5, bf16[1,128,128]{2,1,0:T(8,128)(2,1)} %bitcast.8, bf16[16,128,128]{2,1,0:T(8,128)(2,1)} %bitcast.6), kind=kLoop, calls=%fused_computation | loop fusion | flops 1671168 | bytes 2228224 | tf_op jit(solution)/shard_map/concatenate | solution.py:511
  1.5 1.5 %collective-permute-start = (bf16[34,128,128]{2,1,0:T(8,128)(2,1)S(1)}, bf16[34,128,128]{2,1,0:T(8,128)(2,1)S(1)}, u32[]{:S(2)}, u32[]{:S(2)}) collective-permute-start(bf16[34,128,128]{2,1,0:T(8,128)(2,1)S(1)} %pad_maximum_fusion.refs_2_), channel_id=1, source_target_pairs={{0,16},{8,24},{16,0},{24,8},{32,48},{40,56},{48,32},{56,40},{64,80... | collective-permute-start | bytes 3342344 | tf_op jit(solution)/shard_map/ppermute | solution.py:479
  3.0 1.9 %collective-permute-start.2 = (bf16[128,1024]{1,0:T(8,128)(2,1)}, bf16[128,1024]{1,0:T(8,128)(2,1)}, u32[]{:S(2)}, u32[]{:S(2)}) collective-permute-start(bf16[128,1024]{1,0:T(8,128)(2,1)} %refs_4_.1), channel_id=1, source_target_pairs={{0,32},{8,40},{16,48},{24,56},{32,64},{40,72},{48,80},{56,88},{64,... | collective-permute-start | bytes 786440 | tf_op jit(solution)/shard_map/ppermute | solution.py:484
  4.9 2.1 %collective-permute-start.4 = (bf16[128,1024]{1,0:T(8,128)(2,1)}, bf16[128,1024]{1,0:T(8,128)(2,1)}, u32[]{:S(2)}, u32[]{:S(2)}) collective-permute-start(bf16[128,1024]{1,0:T(8,128)(2,1)} %refs_4_.1), channel_id=1, source_target_pairs={{0,96},{8,104},{16,112},{24,120},{32,0},{40,8},{48,16},{56,24},{64... | collective-permute-start | bytes 786440 | tf_op jit(solution)/shard_map/ppermute | solution.py:484
  7.0 1.9 %collective-permute-start.3 = (bf16[128,1024]{1,0:T(8,128)(2,1)}, bf16[128,1024]{1,0:T(8,128)(2,1)}, u32[]{:S(2)}, u32[]{:S(2)}) collective-permute-start(bf16[128,1024]{1,0:T(8,128)(2,1)} %refs_4_.1), channel_id=1, source_target_pairs={{0,64},{8,72},{16,80},{24,88},{32,96},{40,104},{48,112},{56,120},{... | collective-permute-start | bytes 786440 | tf_op jit(solution)/shard_map/ppermute | solution.py:484
  8.9 4.2 %plan.1 = (s32[1152]{0:T(1024)S(4)}, s32[1152]{0:T(1024)S(4)}, s32[1152]{0:T(1024)S(4)}, s32[1152]{0:T(1024)S(4)}) custom-call(s32[1]{0:T(128)} %bitcast.me_ref, s32[4,64]{1,0:T(4,128)} %table_ref.1, s32[4]{0:T(128)} %len_ref.1, s32[5]{0:T(128)} %refs_1_.7), custom_call_target="tpu_custom_call" | custom-call | flops 1000000000 | bytes 100000 | tf_op jit(solution)/shard_map/plan/pallas_call | solution.py:127
  13.1 5.0 %attend_near_own.1 = (bf16[1,128,1024]{2,1,0:T(8,128)(2,1)}, f32[1,128,1024]{2,1,0:T(8,128)}, f32[1,1,1024]{2,1,0:T(1,128)}, f32[1,1,1024]{2,1,0:T(1,128)}) custom-call(s32[1152]{0:T(1024)S(4)} %get-tuple-element.51.refs_0_, s32[5]{0:T(128)S(1)} %copy-done, bf16[34,128,128]{2,1,0:T(8,128)(2,1)S(1)} %pad_maximum_fusion.refs_2_, ...), custom_call_target="tpu_custom_call" | custom-call | flops 2000000000 | bytes 100000 | tf_op jit(solution)/shard_map/attend_near_own/pallas_call | solution.py:413
  18.2 0.7 collective-permute-done.4.refs_6_
  18.9 1.9 %collective-permute-done.3.refs_5_ = bf16[128,1024]{1,0:T(8,128)(2,1)} collective-permute-done((bf16[128,1024]{1,0:T(8,128)(2,1)}, bf16[128,1024]{1,0:T(8,128)(2,1)}, u32[]{:S(2)}, u32[]{:S(2)}) %collective-permute-start.3) | collective-permute-done | bytes 262176 | tf_op jit(solution)/shard_map/ppermute | solution.py:484
  20.7 14.5 %attend_near.1 = (bf16[3,128,1024]{2,1,0:T(8,128)(2,1)}, f32[3,128,1024]{2,1,0:T(8,128)}, f32[3,1,1024]{2,1,0:T(1,128)}, f32[3,1,1024]{2,1,0:T(1,128)}) custom-call(s32[1152]{0:T(1024)S(4)} %get-tuple-element.56.refs_0_, s32[5]{0:T(128)S(1)} %copy-done, bf16[34,128,128]{2,1,0:T(8,128)(2,1)S(1)} %pad_maximum_fusion.refs_2_, ...), custom_call_target="tpu_custom_call" | custom-call | flops 2000000000 | bytes 100000 | tf_op jit(solution)/shard_map/attend_near/pallas_call | solution.py:413
  35.4 2.7 %collective-permute-done.5.refs_3_ = bf16[34,128,128]{2,1,0:T(8,128)(2,1)S(1)} collective-permute-done((bf16[34,128,128]{2,1,0:T(8,128)(2,1)S(1)}, bf16[34,128,128]{2,1,0:T(8,128)(2,1)S(1)}, u32[]{:S(2)}, u32[]{:S(2)}) %collective-permute-start.5) | collective-permute-done | bytes 1114144 | tf_op jit(solution)/shard_map/ppermute | solution.py:479
  38.1 11.4 %attend_far.1 = (bf16[1056,128]{1,0:T(8,128)(2,1)S(1)}, bf16[1056,128]{1,0:T(8,128)(2,1)S(1)}, bf16[1056,128]{1,0:T(8,128)(2,1)S(1)}) custom-call(s32[1152]{0:T(1024)S(4)} %get-tuple-element.49.refs_0_, s32[5]{0:T(128)S(1)} %copy-done, bf16[34,128,128]{2,1,0:T(8,128)(2,1)S(1)} %collective-permute-done.refs_2_, ...), custom_call_target="tpu_custom_call" | custom-call | flops 2000000000 | bytes 100000 | tf_op jit(solution)/shard_map/attend_far/pallas_call | solution.py:413
  49.6 2.7 %collective-permute-start.6 = (bf16[1056,128]{1,0:T(8,128)(2,1)S(1)}, bf16[1056,128]{1,0:T(8,128)(2,1)S(1)}, u32[]{:S(2)}, u32[]{:S(2)}) collective-permute-start(bf16[1056,128]{1,0:T(8,128)(2,1)S(1)} %get-tuple-element.76), channel_id=1, source_target_pairs={{0,64},{8,72},{16,80},{24,88},{32,96},{40,104},{48,112},{56,120},{... | collective-permute-start | bytes 811016 | tf_op jit(solution)/shard_map/ppermute | solution.py:484
  52.3 2.0 %collective-permute-start.8 = (bf16[1056,128]{1,0:T(8,128)(2,1)S(1)}, bf16[1056,128]{1,0:T(8,128)(2,1)S(1)}, u32[]{:S(2)}, u32[]{:S(2)}) collective-permute-start(bf16[1056,128]{1,0:T(8,128)(2,1)S(1)} %get-tuple-element.78), channel_id=1, source_target_pairs={{0,32},{8,40},{16,48},{24,56},{32,64},{40,72},{48,80},{56,88},{64,... | collective-permute-start | bytes 811016 | tf_op jit(solution)/shard_map/ppermute | solution.py:484
  54.4 7.1 %attend_far_own.1 = (bf16[1056,128]{1,0:T(8,128)(2,1)S(1)}, bf16[1024,1024]{1,0:T(8,128)(2,1)S(1)}, bf16[1024,1024]{1,0:T(8,128)(2,1)S(1)}, bf16[1024,1024]{1,0:...) custom-call(s32[1152]{0:T(1024)S(4)} %get-tuple-element.69.refs_0_, ...), custom_call_target="tpu_custom_call" | custom-call | flops 2000000000 | bytes 100000 | tf_op jit(solution)/shard_map/attend_far_own/pallas_call | solution.py:413
  61.7 1.9 %collective-permute-done.8.refs_3_ = bf16[1056,128]{1,0:T(8,128)(2,1)S(1)} collective-permute-done((bf16[1056,128]{1,0:T(8,128)(2,1)S(1)}, bf16[1056,128]{1,0:T(8,128)(2,1)S(1)}, u32[]{:S(2)}, u32[]{:S(2)}) %collective-permute-start.8) | collective-permute-done | bytes 270368 | tf_op jit(solution)/shard_map/ppermute | solution.py:484
  65.4 3.1 %collective-permute-start.10 = (bf16[128,1024]{1,0:T(8,128)(2,1)S(1)}, bf16[128,1024]{1,0:T(8,128)(2,1)S(1)}, u32[]{:S(2)}, u32[]{:S(2)}) collective-permute-start(bf16[128,1024]{1,0:T(8,128)(2,1)S(1)} %project.10), channel_id=1, source_target_pairs={{0,6},{1,7},{2,4},{3,5},{4,2},{5,3},{6,0},{7,1},{8,14},{9,15},{10,... | collective-permute-start | bytes 786440 | tf_op jit(solution)/shard_map/ppermute | solution.py:479
  69.7 2.5 %collective-permute-start.12 = (bf16[128,1024]{1,0:T(8,128)(2,1)S(1)}, bf16[128,1024]{1,0:T(8,128)(2,1)S(1)}, u32[]{:S(2)}, u32[]{:S(2)}) collective-permute-start(bf16[128,1024]{1,0:T(8,128)(2,1)S(1)} %project.12), channel_id=1, source_target_pairs={{0,7},{1,6},{2,5},{3,4},{4,3},{5,2},{6,1},{7,0},{8,15},{9,14},{10,... | collective-permute-start | bytes 786440 | tf_op jit(solution)/shard_map/ppermute | solution.py:479
  72.2 0.8 collective-permute-start.13
  73.9 3.3 %collective-permute-start.14 = (bf16[128,1024]{1,0:T(8,128)(2,1)S(1)}, bf16[128,1024]{1,0:T(8,128)(2,1)S(1)}, u32[]{:S(2)}, u32[]{:S(2)}) collective-permute-start(bf16[128,1024]{1,0:T(8,128)(2,1)S(1)} %project.14), channel_id=1, source_target_pairs={{0,4},{1,5},{2,6},{3,7},{4,0},{5,1},{6,2},{7,3},{8,12},{9,13},{10,... | collective-permute-start | bytes 786440 | tf_op jit(solution)/shard_map/ppermute | solution.py:479
  77.2 4.4 %collective-permute-done.10 = bf16[128,1024]{1,0:T(8,128)(2,1)S(1)} collective-permute-done((bf16[128,1024]{1,0:T(8,128)(2,1)S(1)}, bf16[128,1024]{1,0:T(8,128)(2,1)S(1)}, u32[]{:S(2)}, u32[]{:S(2)}) %collective-permute-start.10) | collective-permute-done | bytes 262176 | tf_op jit(solution)/shard_map/ppermute | solution.py:479
  82.1 3.4 %collective-permute-start.15 = (bf16[128,1024]{1,0:T(8,128)(2,1)S(1)}, bf16[128,1024]{1,0:T(8,128)(2,1)S(1)}, u32[]{:S(2)}, u32[]{:S(2)}) collective-permute-start(bf16[128,1024]{1,0:T(8,128)(2,1)S(1)} %project.15), channel_id=1, source_target_pairs={{0,5},{1,4},{2,7},{3,6},{4,1},{5,0},{6,3},{7,2},{8,13},{9,12},{10,... | collective-permute-start | bytes 786440 | tf_op jit(solution)/shard_map/ppermute | solution.py:479
  85.7 9.2 %collective-permute-done.14 = bf16[128,1024]{1,0:T(8,128)(2,1)S(1)} collective-permute-done((bf16[128,1024]{1,0:T(8,128)(2,1)S(1)}, bf16[128,1024]{1,0:T(8,128)(2,1)S(1)}, u32[]{:S(2)}, u32[]{:S(2)}) %collective-permute-start.14) | collective-permute-done | bytes 262176 | tf_op jit(solution)/shard_map/ppermute | solution.py:479
  94.9 0.8 add_convert_fusion
  (30 shorter events, 4.8 us)
Async XLA Ops:
  1.4 11.7 %collective-permute-start.1 = (bf16[34,128,128]{2,1,0:T(8,128)(2,1)S(1)}, bf16[34,128,128]{2,1,0:T(8,128)(2,1)S(1)}, u32[]{:S(2)}, u32[]{:S(2)}) collective-permute-start(bf16[34,128,128]{2,1,0:T(8,128)(2,1)S(1)} %pad_maximum_fusion.refs_2_), channel_id=1, source_target_pairs={{0,8},{8,0},{16,24},{24,16},{32,40},{40,32},{48,56},{56,48},{64,72... | collective-permute-start | bytes 3342344 | tf_op jit(solution)/shard_map/ppermute | solution.py:479
  1.5 33.8 %collective-permute-start = (bf16[34,128,128]{2,1,0:T(8,128)(2,1)S(1)}, bf16[34,128,128]{2,1,0:T(8,128)(2,1)S(1)}, u32[]{:S(2)}, u32[]{:S(2)}) collective-permute-start(bf16[34,128,128]{2,1,0:T(8,128)(2,1)S(1)} %pad_maximum_fusion.refs_2_), channel_id=1, source_target_pairs={{0,16},{8,24},{16,0},{24,8},{32,48},{40,56},{48,32},{56,40},{64,80... | collective-permute-start | bytes 3342344 | tf_op jit(solution)/shard_map/ppermute | solution.py:479
  3.0 15.2 %collective-permute-start.2 = (bf16[128,1024]{1,0:T(8,128)(2,1)}, bf16[128,1024]{1,0:T(8,128)(2,1)}, u32[]{:S(2)}, u32[]{:S(2)}) collective-permute-start(bf16[128,1024]{1,0:T(8,128)(2,1)} %refs_4_.1), channel_id=1, source_target_pairs={{0,32},{8,40},{16,48},{24,56},{32,64},{40,72},{48,80},{56,88},{64,... | collective-permute-start | bytes 786440 | tf_op jit(solution)/shard_map/ppermute | solution.py:484
  4.9 14.0 %collective-permute-start.4 = (bf16[128,1024]{1,0:T(8,128)(2,1)}, bf16[128,1024]{1,0:T(8,128)(2,1)}, u32[]{:S(2)}, u32[]{:S(2)}) collective-permute-start(bf16[128,1024]{1,0:T(8,128)(2,1)} %refs_4_.1), channel_id=1, source_target_pairs={{0,96},{8,104},{16,112},{24,120},{32,0},{40,8},{48,16},{56,24},{64... | collective-permute-start | bytes 786440 | tf_op jit(solution)/shard_map/ppermute | solution.py:484
  7.0 13.7 %collective-permute-start.3 = (bf16[128,1024]{1,0:T(8,128)(2,1)}, bf16[128,1024]{1,0:T(8,128)(2,1)}, u32[]{:S(2)}, u32[]{:S(2)}) collective-permute-start(bf16[128,1024]{1,0:T(8,128)(2,1)} %refs_4_.1), channel_id=1, source_target_pairs={{0,64},{8,72},{16,80},{24,88},{32,96},{40,104},{48,112},{56,120},{... | collective-permute-start | bytes 786440 | tf_op jit(solution)/shard_map/ppermute | solution.py:484
  8.9 4.2 %copy-start = (s32[5]{0:T(128)S(1)}, s32[5]{0:T(128)}, u32[]{:S(2)}) copy-start(s32[5]{0:T(128)} %refs_1_.7) | copy-start | bytes 64
  35.3 2.8 %collective-permute-start.5 = (bf16[34,128,128]{2,1,0:T(8,128)(2,1)S(1)}, bf16[34,128,128]{2,1,0:T(8,128)(2,1)S(1)}, u32[]{:S(2)}, u32[]{:S(2)}) collective-permute-start(bf16[34,128,128]{2,1,0:T(8,128)(2,1)S(1)} %collective-permute-done.refs_2_), channel_id=1, source_target_pairs={{0,8},{8,0},{16,24},{24,16},{32,40},{40,32},{48,56},{56,48},{64,72... | collective-permute-start | bytes 3342344 | tf_op jit(solution)/shard_map/ppermute | solution.py:479
  38.1 16.2 %copy-start.1 = (s32[8]{0:T(128)S(1)}, s32[8]{0:T(128)}, u32[]{:S(2)}) copy-start(s32[8]{0:T(128)} %constant.11.clone) | copy-start | bytes 100
  49.6 11.9 %collective-permute-start.6 = (bf16[1056,128]{1,0:T(8,128)(2,1)S(1)}, bf16[1056,128]{1,0:T(8,128)(2,1)S(1)}, u32[]{:S(2)}, u32[]{:S(2)}) collective-permute-start(bf16[1056,128]{1,0:T(8,128)(2,1)S(1)} %get-tuple-element.76), channel_id=1, source_target_pairs={{0,64},{8,72},{16,80},{24,88},{32,96},{40,104},{48,112},{56,120},{... | collective-permute-start | bytes 811016 | tf_op jit(solution)/shard_map/ppermute | solution.py:484
  52.3 9.4 %collective-permute-start.7 = (bf16[1056,128]{1,0:T(8,128)(2,1)S(1)}, bf16[1056,128]{1,0:T(8,128)(2,1)S(1)}, u32[]{:S(2)}, u32[]{:S(2)}) collective-permute-start(bf16[1056,128]{1,0:T(8,128)(2,1)S(1)} %get-tuple-element.77), channel_id=1, source_target_pairs={{0,96},{8,104},{16,112},{24,120},{32,0},{40,8},{48,16},{56,24},{64... | collective-permute-start | bytes 811016 | tf_op jit(solution)/shard_map/ppermute | solution.py:484
  52.3 11.3 %collective-permute-start.8 = (bf16[1056,128]{1,0:T(8,128)(2,1)S(1)}, bf16[1056,128]{1,0:T(8,128)(2,1)S(1)}, u32[]{:S(2)}, u32[]{:S(2)}) collective-permute-start(bf16[1056,128]{1,0:T(8,128)(2,1)S(1)} %get-tuple-element.78), channel_id=1, source_target_pairs={{0,32},{8,40},{16,48},{24,56},{32,64},{40,72},{48,80},{56,88},{64,... | collective-permute-start | bytes 811016 | tf_op jit(solution)/shard_map/ppermute | solution.py:484
  64.9 8.6 %collective-permute-start.9 = (bf16[128,1024]{1,0:T(8,128)(2,1)S(1)}, bf16[128,1024]{1,0:T(8,128)(2,1)S(1)}, u32[]{:S(2)}, u32[]{:S(2)}) collective-permute-start(bf16[128,1024]{1,0:T(8,128)(2,1)S(1)} %project.9), channel_id=1, source_target_pairs={{0,1},{1,0},{2,3},{3,2},{4,5},{5,4},{6,7},{7,6},{8,9},{9,8},{10,11... | collective-permute-start | bytes 786440 | tf_op jit(solution)/shard_map/ppermute | solution.py:479
  65.4 16.2 %collective-permute-start.10 = (bf16[128,1024]{1,0:T(8,128)(2,1)S(1)}, bf16[128,1024]{1,0:T(8,128)(2,1)S(1)}, u32[]{:S(2)}, u32[]{:S(2)}) collective-permute-start(bf16[128,1024]{1,0:T(8,128)(2,1)S(1)} %project.10), channel_id=1, source_target_pairs={{0,6},{1,7},{2,4},{3,5},{4,2},{5,3},{6,0},{7,1},{8,14},{9,15},{10,... | collective-permute-start | bytes 786440 | tf_op jit(solution)/shard_map/ppermute | solution.py:479
  69.4 16.0 %collective-permute-start.11 = (bf16[128,1024]{1,0:T(8,128)(2,1)S(1)}, bf16[128,1024]{1,0:T(8,128)(2,1)S(1)}, u32[]{:S(2)}, u32[]{:S(2)}) collective-permute-start(bf16[128,1024]{1,0:T(8,128)(2,1)S(1)} %project.11), channel_id=1, source_target_pairs={{0,2},{1,3},{2,0},{3,1},{4,6},{5,7},{6,4},{7,5},{8,10},{9,11},{10,... | collective-permute-start | bytes 786440 | tf_op jit(solution)/shard_map/ppermute | solution.py:479
  69.7 15.8 %collective-permute-start.12 = (bf16[128,1024]{1,0:T(8,128)(2,1)S(1)}, bf16[128,1024]{1,0:T(8,128)(2,1)S(1)}, u32[]{:S(2)}, u32[]{:S(2)}) collective-permute-start(bf16[128,1024]{1,0:T(8,128)(2,1)S(1)} %project.12), channel_id=1, source_target_pairs={{0,7},{1,6},{2,5},{3,4},{4,3},{5,2},{6,1},{7,0},{8,15},{9,14},{10,... | collective-permute-start | bytes 786440 | tf_op jit(solution)/shard_map/ppermute | solution.py:479
  72.2 13.3 %collective-permute-start.13 = (bf16[128,1024]{1,0:T(8,128)(2,1)S(1)}, bf16[128,1024]{1,0:T(8,128)(2,1)S(1)}, u32[]{:S(2)}, u32[]{:S(2)}) collective-permute-start(bf16[128,1024]{1,0:T(8,128)(2,1)S(1)} %project.13), channel_id=1, source_target_pairs={{0,3},{1,2},{2,1},{3,0},{4,7},{5,6},{6,5},{7,4},{8,11},{9,10},{10,... | collective-permute-start | bytes 786440 | tf_op jit(solution)/shard_map/ppermute | solution.py:479
  73.9 21.0 %collective-permute-start.14 = (bf16[128,1024]{1,0:T(8,128)(2,1)S(1)}, bf16[128,1024]{1,0:T(8,128)(2,1)S(1)}, u32[]{:S(2)}, u32[]{:S(2)}) collective-permute-start(bf16[128,1024]{1,0:T(8,128)(2,1)S(1)} %project.14), channel_id=1, source_target_pairs={{0,4},{1,5},{2,6},{3,7},{4,0},{5,1},{6,2},{7,3},{8,12},{9,13},{10,... | collective-permute-start | bytes 786440 | tf_op jit(solution)/shard_map/ppermute | solution.py:479
  82.1 12.8 %collective-permute-start.15 = (bf16[128,1024]{1,0:T(8,128)(2,1)S(1)}, bf16[128,1024]{1,0:T(8,128)(2,1)S(1)}, u32[]{:S(2)}, u32[]{:S(2)}) collective-permute-start(bf16[128,1024]{1,0:T(8,128)(2,1)S(1)} %project.15), channel_id=1, source_target_pairs={{0,5},{1,4},{2,7},{3,6},{4,1},{5,0},{6,3},{7,2},{8,13},{9,12},{10,... | collective-permute-start | bytes 786440 | tf_op jit(solution)/shard_map/ppermute | solution.py:479
where the time goes:
time: 96.9 us; the launch traced here: 95.7 us
  Pallas kernels  46.2 us (48%)
  starting transfers between devices  25.7 us (27%)
  waiting for transfers between devices  21.1 us (22%)
  other arithmetic  2.41 us (2%)
    pallas_call x4, Pallas kernels, attend(): pl.pallas_call(functools.partial(attend_kernel, form), out_shape=out_shap...  38.2 us
    ppermute x10, waiting for transfers between devices, swap(): lax.ppermute(value, axis, [(i, i ^ mask) for i in range(lax.axis_size(axi...  16.4 us
    ppermute x10, starting transfers between devices, swap(): lax.ppermute(value, axis, [(i, i ^ mask) for i in range(lax.axis_size(axi...  15.1 us
    ppermute x6, starting transfers between devices, forward(): lax.ppermute(value, axis, [(i, (i + by) % count) for i in range(count)])  10.7 us
    ppermute x6, waiting for transfers between devices, forward(): lax.ppermute(value, axis, [(i, (i + by) % count) for i in range(count)])  4.73 us
    pallas_call x1, Pallas kernels, make_plan(): pl.pallas_call(functools.partial(plan_kernel, requests, blocks, page_size...  4.2 us
    pallas_call x8, Pallas kernels, project(): pl.pallas_call(project_kernel, out_shape=jax.ShapeDtypeStruct((rows, wide...  3.57 us
  transfers between devices with their start and end apart: 16, of which 7 were waited for; matrix products, arithmetic and copies ran while one was open for 0% of the time, Pallas kernels for 35%

commit v1 on v0

--- a/solution.py
+++ b/solution.py
@@ -455,24 +455,29 @@
     )(*messages)
 
 
-def project_kernel(x_ref, w_ref, out_ref):
-    out_ref[...] = jnp.dot(x_ref[...], w_ref[...], preferred_element_type=F32).astype(out_ref.dtype)
-
-
-def project(attended, weight, dtype):
+def project_kernel(x_ref, *refs):
+    weight_refs, out_ref = refs[:-1], refs[-1]
+    wide = weight_refs[0].shape[1]
+    for n, w_ref in enumerate(weight_refs):
+        out_ref[:, n * wide : (n + 1) * wide] = jnp.dot(
+            x_ref[...], w_ref[...], preferred_element_type=F32
+        ).astype(out_ref.dtype)
+
+
+def project(attended, weights, dtype):
     rows, depth = attended.shape
-    wide = weight.shape[1]
+    wide = weights[0].shape[1] * len(weights)
     return pl.pallas_call(
         project_kernel,
         out_shape=jax.ShapeDtypeStruct((rows, wide), dtype),
-        in_specs=[vmem()] * 2,
+        in_specs=[vmem()] * (1 + len(weights)),
         out_specs=vmem(),
         compiler_params=pltpu.CompilerParams(vmem_limit_bytes=SMALL_VMEM_BYTES),
         cost_estimate=pl.CostEstimate(
             flops=2 * rows * depth * wide, bytes_accessed=2 * depth * wide, transcendentals=0
         ),
         name="project",
-    )(attended, weight)
+    )(attended, *weights)
 
 
 def swap(value, axis, mask):
@@ -502,7 +507,7 @@
     page_size, head_width = paged_key_cache.shape[2:]
     scale = math.log2(math.e) / math.sqrt(head_width)
     wide = out_weight.shape[1] // head_count
-    masks = (1, 6, 2, 7, 3, 4, 5)
+    masks = (2, 3, 6, 7, 5, 4, 1)
     me = position.astype(I32).reshape(1)
 
     def as_blocks(value):
@@ -533,18 +538,18 @@
     received = [message] + [forward(m, "ctx", -4 * k) for k, m in zip((2, 1, 3), [messages[1], messages[0], messages[2]])]
 
     attended = merge(received, queries.shape[1] // head_width)
-    shares = {}
-    for mask, weight, after in zip(masks, weights, (None,) * 5 + masks[:2]):
-        given = attended
-        if after:
-            given, shares[after] = lax.optimization_barrier((attended, shares[after]))
-        shares[mask] = swap(project(given, weight, BF16), "head", mask)
-    total = project(attended, weights[-1], F32)
-    for mask in masks[:5]:
-        total = total + shares[mask].astype(F32)
+    sides = []
+    for n in (0, 2):
+        sides.append(swap(project(attended, weights[n : n + 2], BF16), "head", masks[n]))
+    across = swap(project(attended, weights[4:5], BF16), "head", 1)
+    opposite, cross, total = (project(attended, [w], F32) for w in weights[5:8])
+    sides[0], across = lax.optimization_barrier((sides[0], across))
+    opposite = swap((opposite + across.astype(F32)).astype(BF16), "head", 4)
+    cross = cross + sides[0][:, wide:].astype(F32) + sides[1][:, wide:].astype(F32)
+    cross = swap(cross.astype(BF16), "head", 1)
+    total = total + sides[0][:, :wide].astype(F32) + sides[1][:, :wide].astype(F32)
     total = lax.optimization_barrier(total)
-    for mask in masks[5:]:
-        total = total + shares[mask].astype(F32)
+    total = total + opposite.astype(F32) + cross.astype(F32)
     return total.astype(BF16)
 
 

time: 96.9 us -> 90.8 us (0.937)
  the two profiles are of different devices: /device:TPU:6 before, /device:TPU:0 now
where the time goes in v1:
time: 90.8 us; the launch traced here: 91.1 us
  Pallas kernels  44.1 us (49%)
  waiting for transfers between devices  24.3 us (27%)
  starting transfers between devices  20 us (22%)
  other arithmetic  2.47 us (3%)
    pallas_call x4, Pallas kernels, attend(): pl.pallas_call(functools.partial(attend_kernel, form), out_shape=out_shap...  36.4 us
    ppermute x8, waiting for transfers between devices, swap(): lax.ppermute(value, axis, [(i, i ^ mask) for i in range(lax.axis_size(axi...  16.3 us
    ppermute x8, starting transfers between devices, swap(): lax.ppermute(value, axis, [(i, i ^ mask) for i in range(lax.axis_size(axi...  11.9 us
    ppermute x6, waiting for transfers between devices, forward(): lax.ppermute(value, axis, [(i, (i + by) % count) for i in range(count)])  8.09 us
    ppermute x6, starting transfers between devices, forward(): lax.ppermute(value, axis, [(i, (i + by) % count) for i in range(count)])  8.08 us
    pallas_call x1, Pallas kernels, make_plan(): pl.pallas_call(functools.partial(plan_kernel, requests, blocks, page_size...  4.2 us
    pallas_call x6, Pallas kernels, project(): pl.pallas_call(project_kernel, out_shape=jax.ShapeDtypeStruct((rows, wide...  3.22 us
  transfers between devices with their start and end apart: 14, of which 8 were waited for; matrix products, arithmetic and copies ran while one was open for 0% of the time, Pallas kernels for 38%

profile of v1, /device:TPU:0, one launch (start us, length us, event | category | flops | bytes accessed | tf_op | source)
XLA Modules:
  0.0 91.1 jit_solution(17400066891673024447)
XLA Ops:
  0.0 1.4 %pad_maximum_fusion.refs_2_ = bf16[34,128,128]{2,1,0:T(8,128)(2,1)S(1)} fusion(bf16[1,128,128]{2,1,0:T(8,128)(2,1)} %bitcast.7, bf16[16,128,128]{2,1,0:T(8,128)(2,1)} %bitcast.5, bf16[1,128,128]{2,1,0:T(8,128)(2,1)} %bitcast.8, bf16[16,128,128]{2,1,0:T(8,128)(2,1)} %bitcast.6), kind=kLoop, calls=%fused_computation | loop fusion | flops 1671168 | bytes 2228224 | tf_op jit(solution)/shard_map/concatenate | solution.py:516
  1.5 3.2 %collective-permute-start = (bf16[34,128,128]{2,1,0:T(8,128)(2,1)S(1)}, bf16[34,128,128]{2,1,0:T(8,128)(2,1)S(1)}, u32[]{:S(2)}, u32[]{:S(2)}) collective-permute-start(bf16[34,128,128]{2,1,0:T(8,128)(2,1)S(1)} %pad_maximum_fusion.refs_2_), channel_id=1, source_target_pairs={{0,16},{8,24},{16,0},{24,8},{32,48},{40,56},{48,32},{56,40},{64,80... | collective-permute-start | bytes 3342344 | tf_op jit(solution)/shard_map/ppermute | solution.py:484
  4.7 1.9 %collective-permute-start.2 = (bf16[128,1024]{1,0:T(8,128)(2,1)}, bf16[128,1024]{1,0:T(8,128)(2,1)}, u32[]{:S(2)}, u32[]{:S(2)}) collective-permute-start(bf16[128,1024]{1,0:T(8,128)(2,1)} %refs_4_.1), channel_id=1, source_target_pairs={{0,32},{8,40},{16,48},{24,56},{32,64},{40,72},{48,80},{56,88},{64,... | collective-permute-start | bytes 786440 | tf_op jit(solution)/shard_map/ppermute | solution.py:489
  6.6 2.1 %collective-permute-start.4 = (bf16[128,1024]{1,0:T(8,128)(2,1)}, bf16[128,1024]{1,0:T(8,128)(2,1)}, u32[]{:S(2)}, u32[]{:S(2)}) collective-permute-start(bf16[128,1024]{1,0:T(8,128)(2,1)} %refs_4_.1), channel_id=1, source_target_pairs={{0,96},{8,104},{16,112},{24,120},{32,0},{40,8},{48,16},{56,24},{64... | collective-permute-start | bytes 786440 | tf_op jit(solution)/shard_map/ppermute | solution.py:489
  8.7 1.9 %collective-permute-start.3 = (bf16[128,1024]{1,0:T(8,128)(2,1)}, bf16[128,1024]{1,0:T(8,128)(2,1)}, u32[]{:S(2)}, u32[]{:S(2)}) collective-permute-start(bf16[128,1024]{1,0:T(8,128)(2,1)} %refs_4_.1), channel_id=1, source_target_pairs={{0,64},{8,72},{16,80},{24,88},{32,96},{40,104},{48,112},{56,120},{... | collective-permute-start | bytes 786440 | tf_op jit(solution)/shard_map/ppermute | solution.py:489
  10.6 4.2 %plan.1 = (s32[1152]{0:T(1024)S(4)}, s32[1152]{0:T(1024)S(4)}, s32[1152]{0:T(1024)S(4)}, s32[1152]{0:T(1024)S(4)}) custom-call(s32[1]{0:T(128)} %bitcast.me_ref, s32[4,64]{1,0:T(4,128)} %table_ref.1, s32[4]{0:T(128)} %len_ref.1, s32[5]{0:T(128)} %refs_1_.7), custom_call_target="tpu_custom_call" | custom-call | flops 1000000000 | bytes 100000 | tf_op jit(solution)/shard_map/plan/pallas_call | solution.py:127
  14.8 6.8 %attend_near_own.1 = (bf16[1,128,1024]{2,1,0:T(8,128)(2,1)}, f32[1,128,1024]{2,1,0:T(8,128)}, f32[1,1,1024]{2,1,0:T(1,128)}, f32[1,1,1024]{2,1,0:T(1,128)}) custom-call(s32[1152]{0:T(1024)S(4)} %get-tuple-element.49.refs_0_, s32[5]{0:T(128)S(1)} %copy-done, bf16[34,128,128]{2,1,0:T(8,128)(2,1)S(1)} %pad_maximum_fusion.refs_2_, ...), custom_call_target="tpu_custom_call" | custom-call | flops 2000000000 | bytes 100000 | tf_op jit(solution)/shard_map/attend_near_own/pallas_call | solution.py:413
  21.7 0.8 collective-permute-done.3.refs_5_
  22.4 14.1 %attend_near.1 = (bf16[3,128,1024]{2,1,0:T(8,128)(2,1)}, f32[3,128,1024]{2,1,0:T(8,128)}, f32[3,1,1024]{2,1,0:T(1,128)}, f32[3,1,1024]{2,1,0:T(1,128)}) custom-call(s32[1152]{0:T(1024)S(4)} %get-tuple-element.54.refs_0_, s32[5]{0:T(128)S(1)} %copy-done, bf16[34,128,128]{2,1,0:T(8,128)(2,1)S(1)} %pad_maximum_fusion.refs_2_, ...), custom_call_target="tpu_custom_call" | custom-call | flops 2000000000 | bytes 100000 | tf_op jit(solution)/shard_map/attend_near/pallas_call | solution.py:413
  36.7 2.7 %collective-permute-done.5.refs_3_ = bf16[34,128,128]{2,1,0:T(8,128)(2,1)S(1)} collective-permute-done((bf16[34,128,128]{2,1,0:T(8,128)(2,1)S(1)}, bf16[34,128,128]{2,1,0:T(8,128)(2,1)S(1)}, u32[]{:S(2)}, u32[]{:S(2)}) %collective-permute-start.5) | collective-permute-done | bytes 1114144 | tf_op jit(solution)/shard_map/ppermute | solution.py:484
  39.4 8.3 %attend_far.1 = (bf16[1056,128]{1,0:T(8,128)(2,1)S(1)}, bf16[1056,128]{1,0:T(8,128)(2,1)S(1)}, bf16[1056,128]{1,0:T(8,128)(2,1)S(1)}) custom-call(s32[1152]{0:T(1024)S(4)} %get-tuple-element.47.refs_0_, s32[5]{0:T(128)S(1)} %copy-done, bf16[34,128,128]{2,1,0:T(8,128)(2,1)S(1)} %collective-permute-done.refs_2_, ...), custom_call_target="tpu_custom_call" | custom-call | flops 2000000000 | bytes 100000 | tf_op jit(solution)/shard_map/attend_far/pallas_call | solution.py:413
  47.8 1.8 %collective-permute-start.7 = (bf16[1056,128]{1,0:T(8,128)(2,1)S(1)}, bf16[1056,128]{1,0:T(8,128)(2,1)S(1)}, u32[]{:S(2)}, u32[]{:S(2)}) collective-permute-start(bf16[1056,128]{1,0:T(8,128)(2,1)S(1)} %get-tuple-element.75), channel_id=1, source_target_pairs={{0,96},{8,104},{16,112},{24,120},{32,0},{40,8},{48,16},{56,24},{64... | collective-permute-start | bytes 811016 | tf_op jit(solution)/shard_map/ppermute | solution.py:489
  50.0 7.1 %attend_far_own.1 = (bf16[1056,128]{1,0:T(8,128)(2,1)S(1)}, bf16[1024,1024]{1,0:T(8,128)(2,1)S(1)}, bf16[1024,1024]{1,0:T(8,128)(2,1)S(1)}, bf16[1024,1024]{1,0:...) custom-call(s32[1152]{0:T(1024)S(4)} %get-tuple-element.67.refs_0_, ...), custom_call_target="tpu_custom_call" | custom-call | flops 2000000000 | bytes 100000 | tf_op jit(solution)/shard_map/attend_far_own/pallas_call | solution.py:413
  57.1 3.0 %collective-permute-done.7.refs_2_ = bf16[1056,128]{1,0:T(8,128)(2,1)S(1)} collective-permute-done((bf16[1056,128]{1,0:T(8,128)(2,1)S(1)}, bf16[1056,128]{1,0:T(8,128)(2,1)S(1)}, u32[]{:S(2)}, u32[]{:S(2)}) %collective-permute-start.7) | collective-permute-done | bytes 270368 | tf_op jit(solution)/shard_map/ppermute | solution.py:489
  60.1 4.2 %collective-permute-done.8.refs_3_ = bf16[1056,128]{1,0:T(8,128)(2,1)S(1)} collective-permute-done((bf16[1056,128]{1,0:T(8,128)(2,1)S(1)}, bf16[1056,128]{1,0:T(8,128)(2,1)S(1)}, u32[]{:S(2)}, u32[]{:S(2)}) %collective-permute-start.8) | collective-permute-done | bytes 270368 | tf_op jit(solution)/shard_map/ppermute | solution.py:489
  64.7 0.7 project.7
  65.4 1.7 %collective-permute-start.9 = (bf16[128,2048]{1,0:T(8,128)(2,1)S(1)}, bf16[128,2048]{1,0:T(8,128)(2,1)S(1)}, u32[]{:S(2)}, u32[]{:S(2)}) collective-permute-start(bf16[128,2048]{1,0:T(8,128)(2,1)S(1)} %project.7), channel_id=1, source_target_pairs={{0,2},{1,3},{2,0},{3,1},{4,6},{5,7},{6,4},{7,5},{8,10},{9,11},{10,... | collective-permute-start | bytes 1572872 | tf_op jit(solution)/shard_map/ppermute | solution.py:484
  67.8 2.3 %collective-permute-start.11 = (bf16[128,2048]{1,0:T(8,128)(2,1)S(1)}, bf16[128,2048]{1,0:T(8,128)(2,1)S(1)}, u32[]{:S(2)}, u32[]{:S(2)}) collective-permute-start(bf16[128,2048]{1,0:T(8,128)(2,1)S(1)} %project.9), channel_id=1, source_target_pairs={{0,6},{1,7},{2,4},{3,5},{4,2},{5,3},{6,0},{7,1},{8,14},{9,15},{10,... | collective-permute-start | bytes 1572872 | tf_op jit(solution)/shard_map/ppermute | solution.py:484
  72.6 5.8 %collective-permute-done.10 = bf16[128,1024]{1,0:T(8,128)(2,1)S(1)} collective-permute-done((bf16[128,1024]{1,0:T(8,128)(2,1)S(1)}, bf16[128,1024]{1,0:T(8,128)(2,1)S(1)}, u32[]{:S(2)}, u32[]{:S(2)}) %collective-permute-start.10) | collective-permute-done | bytes 262176 | tf_op jit(solution)/shard_map/ppermute | solution.py:484
  78.4 1.1 %collective-permute-done.9 = bf16[128,2048]{1,0:T(8,128)(2,1)S(1)} collective-permute-done((bf16[128,2048]{1,0:T(8,128)(2,1)S(1)}, bf16[128,2048]{1,0:T(8,128)(2,1)S(1)}, u32[]{:S(2)}, u32[]{:S(2)}) %collective-permute-start.9) | collective-permute-done | bytes 524320 | tf_op jit(solution)/shard_map/ppermute | solution.py:484
  79.5 3.3 %collective-permute-start.12 = (bf16[128,1024]{1,0:T(8,128)(2,1)S(1)}, bf16[128,1024]{1,0:T(8,128)(2,1)S(1)}, u32[]{:S(2)}, u32[]{:S(2)}) collective-permute-start(bf16[128,1024]{1,0:T(8,128)(2,1)S(1)} %add_convert_fusion.2), channel_id=1, source_target_pairs={{0,4},{1,5},{2,6},{3,7},{4,0},{5,1},{6,2},{7,3},{8,12},{9,13},{10,... | collective-permute-start | bytes 786440 | tf_op jit(solution)/shard_map/ppermute | solution.py:484
  83.7 4.9 %collective-permute-done.12 = bf16[128,1024]{1,0:T(8,128)(2,1)S(1)} collective-permute-done((bf16[128,1024]{1,0:T(8,128)(2,1)S(1)}, bf16[128,1024]{1,0:T(8,128)(2,1)S(1)}, u32[]{:S(2)}, u32[]{:S(2)}) %collective-permute-start.12) | collective-permute-done | bytes 262176 | tf_op jit(solution)/shard_map/ppermute | solution.py:484
  88.6 1.7 %collective-permute-done.13 = bf16[128,1024]{1,0:T(8,128)(2,1)S(1)} collective-permute-done((bf16[128,1024]{1,0:T(8,128)(2,1)S(1)}, bf16[128,1024]{1,0:T(8,128)(2,1)S(1)}, u32[]{:S(2)}, u32[]{:S(2)}) %collective-permute-start.13) | collective-permute-done | bytes 262176 | tf_op jit(solution)/shard_map/ppermute | solution.py:484
  90.3 0.8 add_convert_fusion
  (25 shorter events, 5.0 us)
Async XLA Ops:
  1.4 13.4 %collective-permute-start.1 = (bf16[34,128,128]{2,1,0:T(8,128)(2,1)S(1)}, bf16[34,128,128]{2,1,0:T(8,128)(2,1)S(1)}, u32[]{:S(2)}, u32[]{:S(2)}) collective-permute-start(bf16[34,128,128]{2,1,0:T(8,128)(2,1)S(1)} %pad_maximum_fusion.refs_2_), channel_id=1, source_target_pairs={{0,8},{8,0},{16,24},{24,16},{32,40},{40,32},{48,56},{56,48},{64,72... | collective-permute-start | bytes 3342344 | tf_op jit(solution)/shard_map/ppermute | solution.py:484
  1.5 35.1 %collective-permute-start = (bf16[34,128,128]{2,1,0:T(8,128)(2,1)S(1)}, bf16[34,128,128]{2,1,0:T(8,128)(2,1)S(1)}, u32[]{:S(2)}, u32[]{:S(2)}) collective-permute-start(bf16[34,128,128]{2,1,0:T(8,128)(2,1)S(1)} %pad_maximum_fusion.refs_2_), channel_id=1, source_target_pairs={{0,16},{8,24},{16,0},{24,8},{32,48},{40,56},{48,32},{56,40},{64,80... | collective-permute-start | bytes 3342344 | tf_op jit(solution)/shard_map/ppermute | solution.py:484
  4.7 17.0 %collective-permute-start.2 = (bf16[128,1024]{1,0:T(8,128)(2,1)}, bf16[128,1024]{1,0:T(8,128)(2,1)}, u32[]{:S(2)}, u32[]{:S(2)}) collective-permute-start(bf16[128,1024]{1,0:T(8,128)(2,1)} %refs_4_.1), channel_id=1, source_target_pairs={{0,32},{8,40},{16,48},{24,56},{32,64},{40,72},{48,80},{56,88},{64,... | collective-permute-start | bytes 786440 | tf_op jit(solution)/shard_map/ppermute | solution.py:489
  6.6 15.1 %collective-permute-start.4 = (bf16[128,1024]{1,0:T(8,128)(2,1)}, bf16[128,1024]{1,0:T(8,128)(2,1)}, u32[]{:S(2)}, u32[]{:S(2)}) collective-permute-start(bf16[128,1024]{1,0:T(8,128)(2,1)} %refs_4_.1), channel_id=1, source_target_pairs={{0,96},{8,104},{16,112},{24,120},{32,0},{40,8},{48,16},{56,24},{64... | collective-permute-start | bytes 786440 | tf_op jit(solution)/shard_map/ppermute | solution.py:489
  8.7 13.7 %collective-permute-start.3 = (bf16[128,1024]{1,0:T(8,128)(2,1)}, bf16[128,1024]{1,0:T(8,128)(2,1)}, u32[]{:S(2)}, u32[]{:S(2)}) collective-permute-start(bf16[128,1024]{1,0:T(8,128)(2,1)} %refs_4_.1), channel_id=1, source_target_pairs={{0,64},{8,72},{16,80},{24,88},{32,96},{40,104},{48,112},{56,120},{... | collective-permute-start | bytes 786440 | tf_op jit(solution)/shard_map/ppermute | solution.py:489
  10.6 4.2 %copy-start = (s32[5]{0:T(128)S(1)}, s32[5]{0:T(128)}, u32[]{:S(2)}) copy-start(s32[5]{0:T(128)} %refs_1_.7) | copy-start | bytes 64
  36.6 2.8 %collective-permute-start.5 = (bf16[34,128,128]{2,1,0:T(8,128)(2,1)S(1)}, bf16[34,128,128]{2,1,0:T(8,128)(2,1)S(1)}, u32[]{:S(2)}, u32[]{:S(2)}) collective-permute-start(bf16[34,128,128]{2,1,0:T(8,128)(2,1)S(1)} %collective-permute-done.refs_2_), channel_id=1, source_target_pairs={{0,8},{8,0},{16,24},{24,16},{32,40},{40,32},{48,56},{56,48},{64,72... | collective-permute-start | bytes 3342344 | tf_op jit(solution)/shard_map/ppermute | solution.py:484
  39.4 10.5 %copy-start.1 = (s32[8]{0:T(128)S(1)}, s32[8]{0:T(128)}, u32[]{:S(2)}) copy-start(s32[8]{0:T(128)} %constant.11.clone) | copy-start | bytes 100
  47.8 9.3 %collective-permute-start.6 = (bf16[1056,128]{1,0:T(8,128)(2,1)S(1)}, bf16[1056,128]{1,0:T(8,128)(2,1)S(1)}, u32[]{:S(2)}, u32[]{:S(2)}) collective-permute-start(bf16[1056,128]{1,0:T(8,128)(2,1)S(1)} %get-tuple-element.74), channel_id=1, source_target_pairs={{0,64},{8,72},{16,80},{24,88},{32,96},{40,104},{48,112},{56,120},{... | collective-permute-start | bytes 811016 | tf_op jit(solution)/shard_map/ppermute | solution.py:489
  47.8 12.3 %collective-permute-start.7 = (bf16[1056,128]{1,0:T(8,128)(2,1)S(1)}, bf16[1056,128]{1,0:T(8,128)(2,1)S(1)}, u32[]{:S(2)}, u32[]{:S(2)}) collective-permute-start(bf16[1056,128]{1,0:T(8,128)(2,1)S(1)} %get-tuple-element.75), channel_id=1, source_target_pairs={{0,96},{8,104},{16,112},{24,120},{32,0},{40,8},{48,16},{56,24},{64... | collective-permute-start | bytes 811016 | tf_op jit(solution)/shard_map/ppermute | solution.py:489
  49.6 14.8 %collective-permute-start.8 = (bf16[1056,128]{1,0:T(8,128)(2,1)S(1)}, bf16[1056,128]{1,0:T(8,128)(2,1)S(1)}, u32[]{:S(2)}, u32[]{:S(2)}) collective-permute-start(bf16[1056,128]{1,0:T(8,128)(2,1)S(1)} %get-tuple-element.76), channel_id=1, source_target_pairs={{0,32},{8,40},{16,48},{24,56},{32,64},{40,72},{48,80},{56,88},{64,... | collective-permute-start | bytes 811016 | tf_op jit(solution)/shard_map/ppermute | solution.py:489
  65.4 14.0 %collective-permute-start.9 = (bf16[128,2048]{1,0:T(8,128)(2,1)S(1)}, bf16[128,2048]{1,0:T(8,128)(2,1)S(1)}, u32[]{:S(2)}, u32[]{:S(2)}) collective-permute-start(bf16[128,2048]{1,0:T(8,128)(2,1)S(1)} %project.7), channel_id=1, source_target_pairs={{0,2},{1,3},{2,0},{3,1},{4,6},{5,7},{6,4},{7,5},{8,10},{9,11},{10,... | collective-permute-start | bytes 1572872 | tf_op jit(solution)/shard_map/ppermute | solution.py:484
  67.8 15.0 %collective-permute-start.11 = (bf16[128,2048]{1,0:T(8,128)(2,1)S(1)}, bf16[128,2048]{1,0:T(8,128)(2,1)S(1)}, u32[]{:S(2)}, u32[]{:S(2)}) collective-permute-start(bf16[128,2048]{1,0:T(8,128)(2,1)S(1)} %project.9), channel_id=1, source_target_pairs={{0,6},{1,7},{2,4},{3,5},{4,2},{5,3},{6,0},{7,1},{8,14},{9,15},{10,... | collective-permute-start | bytes 1572872 | tf_op jit(solution)/shard_map/ppermute | solution.py:484
  70.5 7.8 %collective-permute-start.10 = (bf16[128,1024]{1,0:T(8,128)(2,1)S(1)}, bf16[128,1024]{1,0:T(8,128)(2,1)S(1)}, u32[]{:S(2)}, u32[]{:S(2)}) collective-permute-start(bf16[128,1024]{1,0:T(8,128)(2,1)S(1)} %project.8), channel_id=1, source_target_pairs={{0,1},{1,0},{2,3},{3,2},{4,5},{5,4},{6,7},{7,6},{8,9},{9,8},{10,11... | collective-permute-start | bytes 786440 | tf_op jit(solution)/shard_map/ppermute | solution.py:484
  79.5 9.1 %collective-permute-start.12 = (bf16[128,1024]{1,0:T(8,128)(2,1)S(1)}, bf16[128,1024]{1,0:T(8,128)(2,1)S(1)}, u32[]{:S(2)}, u32[]{:S(2)}) collective-permute-start(bf16[128,1024]{1,0:T(8,128)(2,1)S(1)} %add_convert_fusion.2), channel_id=1, source_target_pairs={{0,4},{1,5},{2,6},{3,7},{4,0},{5,1},{6,2},{7,3},{8,12},{9,13},{10,... | collective-permute-start | bytes 786440 | tf_op jit(solution)/shard_map/ppermute | solution.py:484
  83.0 7.3 %collective-permute-start.13 = (bf16[128,1024]{1,0:T(8,128)(2,1)S(1)}, bf16[128,1024]{1,0:T(8,128)(2,1)S(1)}, u32[]{:S(2)}, u32[]{:S(2)}) collective-permute-start(bf16[128,1024]{1,0:T(8,128)(2,1)S(1)} %get-tuple-element.88), channel_id=1, source_target_pairs={{0,1},{1,0},{2,3},{3,2},{4,5},{5,4},{6,7},{7,6},{8,9},{9,8},{10,11... | collective-permute-start | bytes 786440 | tf_op jit(solution)/shard_map/ppermute | solution.py:484
